TPU v7x, 256 devices: a whole 4x4x8 slice. The times are simulated.
256 devices in a mesh: pb: 64 (over x, z, core), ka: 4 (over y).
Axes of the slice: x: 4, y: 4, z: 8, core: 2. Of those that a mesh axis runs over, the one named last changes fastest.
Arguments:
- query_features: bfloat16 [40960, 256], P('pb', 'ka'), may hold values from -6 to 6
- key_features: bfloat16 [32768, 256], P(('ka', 'pb')), may hold values from -6 to 6
- patch_weight: bfloat16 [64, 64], replicated, may hold values from -0.75 to 0.75
- patch_bias: float32 [64], replicated, may hold values from -4 to 4
- norm_gain: float32 [64], replicated, may hold values from 0.1 to 1.9
- latent_queries: float32 [8, 128], replicated, may hold values from -240 to 240
- key_weight: bfloat16 [64, 128], replicated, may hold values from -0.75 to 0.75
- value_weight: bfloat16 [64, 128], replicated, may hold values from -0.75 to 0.75
- keep_mask: int32 [40960, 512], P('pb', 'ka'), may hold values 0 or 1
Outputs:
- latent_tokens: bfloat16 [40960, 8, 128], P('pb', 'ka')
All inputs are finite; a program needn't handle non-finite values. No bound on the sum of `keep_mask` on one device may be relied on, other than what follows from the above.
Results may differ from a plain program's by a relative error of at most 0.012.
The roundings to bfloat16 on the way count: a program that leaves them out, or rounds other values in their place, can miss the bound.
Values may be sent and summed in bfloat16 or wider, within the bound.
A program may use at most 64 MiB of HBM per device.

v0:
```python
import math

import jax
import jax.numpy as jnp
from jax import lax
from jax.sharding import PartitionSpec as P


def joined(part, axis, combine):
    gathered = jax.tree.map(lambda a: lax.all_gather(a, axis), part)

    def take(source):
        return jax.tree.map(lambda a: lax.dynamic_index_in_dim(a, source, 0, False), gathered)

    return lax.fori_loop(
        1, lax.axis_size(axis), lambda source, state: combine(state, take(source)), take(0)
    )


def combine_parts(first, second):
    top_first, sum_first, val_first = first
    top_second, sum_second, val_second = second
    top_both = jnp.maximum(top_first, top_second)
    fac_first = jnp.exp(top_first - top_both)
    fac_second = jnp.exp(top_second - top_both)
    return (
        top_both,
        sum_first * fac_first + sum_second * fac_second,
        val_first * fac_first[:, :, None] + val_second * fac_second[:, :, None],
    )


def body(
    query_features,
    key_features,
    patch_weight,
    patch_bias,
    norm_gain,
    latent_queries,
    key_weight,
    value_weight,
    keep_mask,
):
    queries = lax.all_gather(query_features, "ka", axis=1, tiled=True)
    key_block = lax.all_gather(key_features, "pb", axis=0, tiled=True)
    n_query = queries.shape[0]
    chans = queries.shape[1]
    n_patch = keep_mask.shape[1]
    n_lat = latent_queries.shape[0]
    lat_dim = latent_queries.shape[1]
    tok_dim = patch_weight.shape[1]
    cell_count = patch_weight.shape[0]
    score_map = jnp.dot(
        key_weight.astype(jnp.float32), latent_queries.T, precision=lax.Precision.HIGHEST
    ) / math.sqrt(lat_dim)
    blk_rows = math.gcd(n_query, 64)
    n_blk = n_query // blk_rows

    def one_block(pair):
        query_rows, mask_rows = pair
        cost_tile = lax.dot_general(
            query_rows, key_block, (((1,), (1,)), ((), ())), preferred_element_type=jnp.float32
        )
        cost_tile = (
            (cost_tile / math.sqrt(chans))
            .astype(jnp.bfloat16)
            .reshape(blk_rows * n_patch, cell_count)
        )
        tokens = jnp.dot(cost_tile, patch_weight, preferred_element_type=jnp.float32).reshape(
            blk_rows, n_patch, tok_dim
        )
        tokens = tokens * mask_rows[:, :, None].astype(jnp.float32) + patch_bias
        centre = jnp.mean(tokens, axis=2, keepdims=True)
        spread = jnp.mean((tokens - centre) ** 2, axis=2, keepdims=True)
        normed = ((tokens - centre) / jnp.sqrt(spread + 1e-05) * norm_gain).astype(jnp.bfloat16)
        normed_f = normed.astype(jnp.float32)
        scores = jnp.einsum("rte,el->rlt", normed_f, score_map, precision=lax.Precision.HIGHEST)
        top_score = jnp.max(scores, axis=2)
        expo = jnp.exp(scores - top_score[:, :, None])
        denom = jnp.sum(expo, axis=2)
        weighted = jnp.einsum("rlt,rte->rle", expo, normed_f, precision=lax.Precision.HIGHEST)
        return (top_score, denom, weighted)

    top_score, denom, weighted = lax.map(
        one_block,
        (queries.reshape(n_blk, blk_rows, chans), keep_mask.reshape(n_blk, blk_rows, n_patch)),
    )
    top_score = top_score.reshape(n_query, n_lat)
    denom = denom.reshape(n_query, n_lat)
    weighted = weighted.reshape(n_query, n_lat, tok_dim)
    per_device = n_lat // lax.axis_size("ka")
    merged_top, merged_sum, merged_val = joined((top_score, denom, weighted), "ka", combine_parts)
    first_lat = lax.axis_index("ka") * per_device
    own_val = lax.dynamic_slice_in_dim(merged_val, first_lat, per_device, 1)
    own_sum = lax.dynamic_slice_in_dim(merged_sum, first_lat, per_device, 1)
    pooled = (own_val / own_sum[:, :, None]).astype(jnp.bfloat16)
    latent = jnp.einsum("rle,ed->rld", pooled, value_weight, preferred_element_type=jnp.float32)
    return latent.astype(jnp.bfloat16)


def solution(mesh):
    placed = (P("pb", "ka"), P(("ka", "pb"), None), P(), P(), P(), P(), P(), P(), P("pb", "ka"))
    return jax.shard_map(
        body, mesh=mesh, in_specs=placed, out_specs=P("pb", "ka", None), check_vma=False
    )
```

profile of v0, /device:TPU:1, one launch (start us, length us, event | category | flops | bytes accessed | tf_op | source)
XLA Modules:
  0.0 325.2 jit_solution(40516366258417011)
XLA Ops:
  7.3 11.9 %all_gather.15 = bf16[640,256]{0,1:T(8,128)(2,1)S(1)} all-gather(bf16[640,64]{0,1:T(8,128)(2,1)} %param.13), channel_id=1, replica_groups=mesh['pb'=64,'ka'=4] {'ka'}, dimensions={1}, use_global_device_ids=true | all-gather | bytes 409600 | tf_op jit(solution)/shard_map/all_gather | solution.py:44
  21.1 72.3 %all-gather.3.cloned.1.call-done = bf16[8192,256]{1,0:T(8,128)(2,1)} async-done(((bf16[128,256]{1,0:T(8,128)(2,1)}), bf16[8192,256]{1,0:T(8,128)(2,1)}) %all-gather.3.cloned.1.call-update) | async-done | bytes 4194320 | tf_op jit(solution)/shard_map/all_gather | solution.py:45
  93.4 126.7 %while.33 = (s32[]{:T(128)}, f32[10,64,8]{2,1,0:T(8,128)}, f32[10,64,8]{2,1,0:T(8,128)}, f32[10,64,8,64]{3,2,1,0:T(8,128)}, bf16[10,64,256]{2,1,0:T(8,128)(2,1)S...) while((s32[]{:T(128)}, f32[10,64,8]{2,1,0:T(8,128)}, ...), condition=%wide.region_5.6_spmd, body=%wide.region_0.5_spmd.sunk | while | flops 442776576 | bytes 19391172 | solution.py:84
  94.1 3.6 %fusion.41 = bf16[64,8192]{1,0:T(8,128)(2,1)S(1)} fusion(bf16[8192,256]{1,0:T(8,128)(2,1)} %get-tuple-element.527, bf16[10,64,256]{2,1,0:T(8,128)(2,1)S(1)} %get-tuple-element.526, s32[]{:T(128)S(6)} %copy.87), kind=kOutput, calls=%fused_computation.1.clone.1 | convolution fusion | flops 269484032 | bytes 5275652 | tf_op jit(solution)/shard_map/while/body/eval_jaxpr/dot_general | solution.py:61
  103.5 2.5 fusion.45
  106.8 3.6 %fusion.41 = bf16[64,8192]{1,0:T(8,128)(2,1)S(1)} fusion(bf16[8192,256]{1,0:T(8,128)(2,1)} %get-tuple-element.527, bf16[10,64,256]{2,1,0:T(8,128)(2,1)S(1)} %get-tuple-element.526, s32[]{:T(128)S(6)} %copy.87), kind=kOutput, calls=%fused_computation.1.clone.1 | convolution fusion | flops 269484032 | bytes 5275652 | tf_op jit(solution)/shard_map/while/body/eval_jaxpr/dot_general | solution.py:61
  116.2 2.5 fusion.45
  119.5 3.6 %fusion.41 = bf16[64,8192]{1,0:T(8,128)(2,1)S(1)} fusion(bf16[8192,256]{1,0:T(8,128)(2,1)} %get-tuple-element.527, bf16[10,64,256]{2,1,0:T(8,128)(2,1)S(1)} %get-tuple-element.526, s32[]{:T(128)S(6)} %copy.87), kind=kOutput, calls=%fused_computation.1.clone.1 | convolution fusion | flops 269484032 | bytes 5275652 | tf_op jit(solution)/shard_map/while/body/eval_jaxpr/dot_general | solution.py:61
  128.9 2.5 fusion.45
  132.2 3.6 %fusion.41 = bf16[64,8192]{1,0:T(8,128)(2,1)S(1)} fusion(bf16[8192,256]{1,0:T(8,128)(2,1)} %get-tuple-element.527, bf16[10,64,256]{2,1,0:T(8,128)(2,1)S(1)} %get-tuple-element.526, s32[]{:T(128)S(6)} %copy.87), kind=kOutput, calls=%fused_computation.1.clone.1 | convolution fusion | flops 269484032 | bytes 5275652 | tf_op jit(solution)/shard_map/while/body/eval_jaxpr/dot_general | solution.py:61
  141.6 2.5 fusion.45
  144.9 3.6 %fusion.41 = bf16[64,8192]{1,0:T(8,128)(2,1)S(1)} fusion(bf16[8192,256]{1,0:T(8,128)(2,1)} %get-tuple-element.527, bf16[10,64,256]{2,1,0:T(8,128)(2,1)S(1)} %get-tuple-element.526, s32[]{:T(128)S(6)} %copy.87), kind=kOutput, calls=%fused_computation.1.clone.1 | convolution fusion | flops 269484032 | bytes 5275652 | tf_op jit(solution)/shard_map/while/body/eval_jaxpr/dot_general | solution.py:61
  154.3 2.5 fusion.45
  157.5 3.6 %fusion.41 = bf16[64,8192]{1,0:T(8,128)(2,1)S(1)} fusion(bf16[8192,256]{1,0:T(8,128)(2,1)} %get-tuple-element.527, bf16[10,64,256]{2,1,0:T(8,128)(2,1)S(1)} %get-tuple-element.526, s32[]{:T(128)S(6)} %copy.87), kind=kOutput, calls=%fused_computation.1.clone.1 | convolution fusion | flops 269484032 | bytes 5275652 | tf_op jit(solution)/shard_map/while/body/eval_jaxpr/dot_general | solution.py:61
  167.0 2.5 fusion.45
  170.2 3.6 %fusion.41 = bf16[64,8192]{1,0:T(8,128)(2,1)S(1)} fusion(bf16[8192,256]{1,0:T(8,128)(2,1)} %get-tuple-element.527, bf16[10,64,256]{2,1,0:T(8,128)(2,1)S(1)} %get-tuple-element.526, s32[]{:T(128)S(6)} %copy.87), kind=kOutput, calls=%fused_computation.1.clone.1 | convolution fusion | flops 269484032 | bytes 5275652 | tf_op jit(solution)/shard_map/while/body/eval_jaxpr/dot_general | solution.py:61
  179.6 2.5 fusion.45
  182.9 3.6 %fusion.41 = bf16[64,8192]{1,0:T(8,128)(2,1)S(1)} fusion(bf16[8192,256]{1,0:T(8,128)(2,1)} %get-tuple-element.527, bf16[10,64,256]{2,1,0:T(8,128)(2,1)S(1)} %get-tuple-element.526, s32[]{:T(128)S(6)} %copy.87), kind=kOutput, calls=%fused_computation.1.clone.1 | convolution fusion | flops 269484032 | bytes 5275652 | tf_op jit(solution)/shard_map/while/body/eval_jaxpr/dot_general | solution.py:61
  195.5 3.6 %fusion.41 = bf16[64,8192]{1,0:T(8,128)(2,1)S(1)} fusion(bf16[8192,256]{1,0:T(8,128)(2,1)} %get-tuple-element.527, bf16[10,64,256]{2,1,0:T(8,128)(2,1)S(1)} %get-tuple-element.526, s32[]{:T(128)S(6)} %copy.87), kind=kOutput, calls=%fused_computation.1.clone.1 | convolution fusion | flops 269484032 | bytes 5275652 | tf_op jit(solution)/shard_map/while/body/eval_jaxpr/dot_general | solution.py:61
  208.2 3.6 %fusion.41 = bf16[64,8192]{1,0:T(8,128)(2,1)S(1)} fusion(bf16[8192,256]{1,0:T(8,128)(2,1)} %get-tuple-element.527, bf16[10,64,256]{2,1,0:T(8,128)(2,1)S(1)} %get-tuple-element.526, s32[]{:T(128)S(6)} %copy.87), kind=kOutput, calls=%fused_computation.1.clone.1 | convolution fusion | flops 269484032 | bytes 5275652 | tf_op jit(solution)/shard_map/while/body/eval_jaxpr/dot_general | solution.py:61
  217.6 2.5 fusion.45
  220.1 3.2 copy.65
  223.6 9.7 %all_gather.17 = f32[4,640,8]{1,2,0:T(8,128)S(1)} all-gather(f32[1,640,8]{1,2,0:T(8,128)S(1)} %copy.71), channel_id=1, replica_groups=mesh['pb'=64,'ka'=4] {'ka'}, dimensions={0}, use_global_device_ids=true | all-gather | bytes 102400 | tf_op jit(solution)/shard_map/all_gather | solution.py:10
  233.3 10.0 %all_gather.18 = f32[4,640,8]{1,2,0:T(8,128)S(1)} all-gather(f32[1,640,8]{1,2,0:T(8,128)S(1)} %copy.72), channel_id=1, replica_groups=mesh['pb'=64,'ka'=4] {'ka'}, dimensions={0}, use_global_device_ids=true | all-gather | bytes 102400 | tf_op jit(solution)/shard_map/all_gather | solution.py:10
  243.4 37.3 %all-gather.5.cloned.1.call-done = f32[4,640,8,64]{1,3,2,0:T(8,128)} async-done(((f32[1,640,8,64]{1,3,2,0:T(8,128)}), f32[4,640,8,64]{1,3,2,0:T(8,128)}) %all-gather.5.cloned.1.call-update) | async-done | bytes 5242896 | tf_op jit(solution)/shard_map/all_gather | solution.py:10
  284.2 30.3 %while.34 = (s32[]{:T(128)}, f32[640,8]{0,1:T(8,128)S(1)}, f32[640,8]{0,1:T(8,128)S(1)}, f32[640,8,64]{2,1,0:T(8,128)}, f32[4,640,8]{1,2,0:T(8,128)S(1)}, /*inde...) while((s32[]{:T(128)}, f32[640,8]{0,1:T(8,128)S(1)}, ...), condition=%wide.region_7.8_spmd, body=%wide.region_6.7_spmd.sunk | while | flops 1013765 | bytes 9461911 | solution.py:15
  284.3 2.6 constant_dynamic-slice_fusion.3
  289.5 4.8 %fusion.47 = f32[640,8,64]{2,1,0:T(8,128)} fusion(f32[1,640,8,64]{3,2,1,0:T(8,128)S(1)} %copy.77, f32[640,8,64]{2,1,0:T(8,128)} %get-tuple-element.547, f32[640,8]{1,0:T(8,128)S(1)} %copy.78, f32[640,8]{1,0:T(8,128)S(1)} %copy.79), kind=kLoop, calls=%fused_computation.22.clone.1 | loop fusion | flops 983040 | bytes 3973120 | tf_op jit(solution)/shard_map/while/body/eval_jaxpr/add | solution.py:29
  294.4 2.6 constant_dynamic-slice_fusion.3
  299.6 4.8 %fusion.47 = f32[640,8,64]{2,1,0:T(8,128)} fusion(f32[1,640,8,64]{3,2,1,0:T(8,128)S(1)} %copy.77, f32[640,8,64]{2,1,0:T(8,128)} %get-tuple-element.547, f32[640,8]{1,0:T(8,128)S(1)} %copy.78, f32[640,8]{1,0:T(8,128)S(1)} %copy.79), kind=kLoop, calls=%fused_computation.22.clone.1 | loop fusion | flops 983040 | bytes 3973120 | tf_op jit(solution)/shard_map/while/body/eval_jaxpr/add | solution.py:29
  304.4 2.6 constant_dynamic-slice_fusion.3
  309.7 4.8 %fusion.47 = f32[640,8,64]{2,1,0:T(8,128)} fusion(f32[1,640,8,64]{3,2,1,0:T(8,128)S(1)} %copy.77, f32[640,8,64]{2,1,0:T(8,128)} %get-tuple-element.547, f32[640,8]{1,0:T(8,128)S(1)} %copy.78, f32[640,8]{1,0:T(8,128)S(1)} %copy.79), kind=kLoop, calls=%fused_computation.22.clone.1 | loop fusion | flops 983040 | bytes 3973120 | tf_op jit(solution)/shard_map/while/body/eval_jaxpr/add | solution.py:29
  (180 shorter events, 88.4 us)
Async XLA Ops:
  6.5 310.5 %copy-start = (bf16[64,128]{1,0:T(8,128)(2,1)S(1)}, bf16[64,128]{1,0:T(8,128)(2,1)}, u32[]{:S(2)}) copy-start(bf16[64,128]{1,0:T(8,128)(2,1)} %param.20) | copy-start | bytes 49156
  6.5 86.8 %all-gather.3.cloned.1.call-start = ((), (), s32[]{:S(2)}) async-start(), calls=%async_computation | async-start | bytes 4259840 | tf_op jit(solution)/shard_map/all_gather | solution.py:45
  7.3 273.4 %all-gather.5.cloned.1.call-start = ((), (), s32[]{:S(2)}) async-start(), calls=%async_computation.1 | async-start | bytes 6553600 | tf_op jit(solution)/shard_map/all_gather | solution.py:10
  97.7 2.3 copy-start.3
  100.9 0.7 copy-start.4
  110.4 2.3 copy-start.3
  113.5 0.7 copy-start.4
  123.1 2.3 copy-start.3
  126.2 0.7 copy-start.4
  135.8 2.3 copy-start.3
  138.9 0.7 copy-start.4
  148.4 2.3 copy-start.3
  151.6 0.7 copy-start.4
  161.1 2.3 copy-start.3
  164.3 0.7 copy-start.4
  173.8 2.3 copy-start.3
  177.0 0.7 copy-start.4
  186.5 2.3 copy-start.3
  189.6 0.7 copy-start.4
  199.1 2.3 copy-start.3
  202.3 0.7 copy-start.4
  211.8 2.3 copy-start.3
  214.9 0.7 copy-start.4
  220.1 3.2 copy-start.1
  220.1 3.4 %copy-start.2 = (f32[10,64,8]{2,1,0:T(8,128)S(1)}, f32[10,64,8]{2,1,0:T(8,128)}, u32[]{:S(2)}) copy-start(f32[10,64,8]{2,1,0:T(8,128)} %get-tuple-element.242) | copy-start | bytes 61444
Sparse Core Ops, SparseCore 0:
  10.1 83.1 all-gather.2
  223.5 57.1 all-gather.4
where the time goes:
time: 327 us; the launch traced here: 325 us
  waiting for transfers between devices  110 us (34%)
  matrix products  76.4 us (23%)
  local copies, waits for them, and re-layouts  58 us (18%)
  other arithmetic  34.4 us (11%)
  blocking collectives  31.7 us (10%)
  between operations  13.5 us (4%)
    all_gather x1, waiting for transfers between devices, body(): key_block = lax.all_gather(key_features, 'pb', axis=0, tiled=True)  72.3 us
    all_gather x1, waiting for transfers between devices, joined(): gathered = jax.tree.map(lambda a: lax.all_gather(a, axis), part)  37.3 us
    dot_general x10, matrix products, one_block(): lax.dot_general(query_rows, key_block, (((1,), (1,)), ((), ())), preferre...  35.6 us
    dot_general x10, matrix products, one_block(): jnp.einsum('rlt,rte->rle', expo, normed_f, precision=lax.Precision.HIGHEST)  25.1 us
    dot_general x10, local copies, waits for them, and re-layouts, one_block(): jnp.dot(cost_tile, patch_weight, preferred_element_type=jnp.float32)  22.9 us
    all_gather x2, blocking collectives, joined(): gathered = jax.tree.map(lambda a: lax.all_gather(a, axis), part)  19.7 us
    dynamic_slice x6, local copies, waits for them, and re-layouts, take(): lax.dynamic_index_in_dim(a, source, 0, False)  14.7 us
    add x3, other arithmetic, combine_parts(): val_first * fac_first[:, :, None] + val_second * fac_second[:, :, None]  14.5 us
  transfers between devices with their start and end apart: 2, of which 2 were waited for; matrix products, arithmetic and copies ran while one was open for 1% of the time, Pallas kernels for 0%

commit v1 on v0

v1 whole, which is shorter than its diff:
```python
import math

import jax
import jax.numpy as jnp
from jax import lax
from jax.experimental import pallas as pl
from jax.experimental.pallas import tpu as pltpu
from jax.sharding import PartitionSpec as P

f32 = jnp.float32
bf16 = jnp.bfloat16
MESH = pl.DeviceIdType.MESH

NX, NZ, NY = 4, 8, 4
NQ, NT, CELLS, CH, E, LAT, LD = 640, 128, 64, 256, 64, 8, 128
NK = NT * CELLS
G = 32
NG = NQ // G
NP = G // 2
CHUNK = 128
NCH = NQ // CHUNK
GPC = CHUNK // G


def dot_nt(a, b):
    return lax.dot_general(a, b, (((1,), (1,)), ((), ())), preferred_element_type=f32)


def gather(me, y, k_ref, q_ref, kbuf, qbuf, ssem, rsem, qssem, qrsem, prepare):
    core = lax.rem(me, 2)
    z = lax.rem(lax.div(me, 2), NZ)
    x = lax.div(me, 2 * NZ)

    def pb(xx, zz, cc):
        return (lax.rem(xx + NX, NX) * NZ + lax.rem(zz + NZ, NZ)) * 2 + cc

    sibling = pb(x, z, 1 - core)
    ring = {"z+": pb(x, z + 1, core), "z-": pb(x, z - 1, core), "x+": pb(x + 1, z, core), "x-": pb(x - 1, z, core)}
    ring["s"] = sibling

    barrier = pltpu.get_barrier_semaphore()
    for other in ring.values():
        pl.semaphore_signal(barrier, inc=1, device_id=(other, y), device_id_type=MESH)
    for o in range(1, NY):
        pl.semaphore_signal(barrier, inc=1, device_id=(me, lax.rem(y + o, NY)), device_id_type=MESH)
    kbuf[me] = k_ref[...]
    qbuf[y] = q_ref[...]
    prepare()
    pl.semaphore_wait(barrier, len(ring) + NY - 1)

    def q_copy(o):
        return pltpu.make_async_remote_copy(
            src_ref=qbuf.at[y], dst_ref=qbuf.at[y], send_sem=qssem.at[o - 1], recv_sem=qrsem.at[o - 1],
            device_id=(me, lax.rem(y + o, NY)), device_id_type=MESH,
        )

    def copy(slot, to, sem):
        return pltpu.make_async_remote_copy(
            src_ref=kbuf.at[slot], dst_ref=kbuf.at[slot], send_sem=ssem.at[sem], recv_sem=rsem.at[slot],
            device_id=(to, y), device_id_type=MESH,
        )

    def run(route):
        count = [0]

        def send(slot, *ways):
            for way in ways:
                copy(slot, ring[way], count[0]).start()
                count[0] += 1

        def arrive(slot):
            copy(slot, sibling, 0).wait_recv()

        route(send, arrive)
        return count[0]

    def z_first(send, arrive):
        zs = [(z, None, 0), (z - 1, "z+", 1), (z + 1, "z-", 1), (z - 2, "z+", 2), (z + 2, "z-", 2), (z - 3, "z+", 3), (z + 3, "z-", 3), (z - 4, "z+", 4)]
        send(me, "z+", "z-", "x+", "x-", "s")
        for k in range(1, NZ + 2):
            if k < NZ:
                zz, way, dist = zs[k]
                slot = pb(x, zz, core)
                arrive(slot)
                if dist < (4 if way == "z+" else 3):
                    send(slot, way)
                send(slot, "x+", "x-", "s")
            if k <= NZ:
                i = k - 1
                slot = pb(x - 1, zs[i][0], core)
                arrive(slot)
                send(slot, *(("x+", "s") if i % 2 == 0 else ("s",)))
                slot = pb(x + 1, zs[i][0], core)
                arrive(slot)
                send(slot, *(("x-", "s") if i % 2 == 1 else ("s",)))
            if k >= 2:
                slot = pb(x + 2, zs[k - 2][0], core)
                arrive(slot)
                send(slot, "s")

    def x_first(send, arrive):
        send(me, "z+", "z-", "x+", "x-", "s")
        xs = [x, x - 1, x + 1, x + 2]
        for i in range(1, NX):
            slot = pb(xs[i], z, core)
            arrive(slot)
            if i == 1:
                send(slot, "x+")
            send(slot, "z+", "z-", "s")
        for dist in range(1, 5):
            for i in range(NX):
                last_plus, last_minus = (4, 3) if i < 2 else (3, 4)
                if dist <= last_plus:
                    slot = pb(xs[i], z - dist, core)
                    arrive(slot)
                    send(slot, *(("z+", "s") if dist < last_plus else ("s",)))
                if dist <= last_minus:
                    slot = pb(xs[i], z + dist, core)
                    arrive(slot)
                    send(slot, *(("z-", "s") if dist < last_minus else ("s",)))

    for o in range(1, NY):
        q_copy(o).start()

    @pl.when(core == 0)
    def _():
        assert run(z_first) == 63

    @pl.when(core == 1)
    def _():
        assert run(x_first) == 63

    @pl.loop(0, NX * NZ)
    def _(i):
        copy(2 * i + 1 - core, sibling, 0).wait_recv()

    for o in range(1, NY):
        q_copy(o).wait()

    @pl.loop(0, 63)
    def _(i):
        copy(me, sibling, i).wait_send()


def order_keys(kbuf, kf_ref, kp_ref):
    @pl.loop(0, NX * NZ * 2)
    def _(s):
        r = pl.multiple_of(s * 128, 128)
        for h in range(2):
            kf_ref[pl.ds(r + h * NK, 128), :] = kbuf[s, :, h * 128 : (h + 1) * 128].astype(f32)

    @pl.loop(0, CELLS)
    def _(c):
        for h in range(2):
            rows = pl.ds(pl.multiple_of(c * NT, NT), NT)
            kp_ref[rows, h * 128 : (h + 1) * 128] = kf_ref[pl.ds(c + h * NK, NT, stride=CELLS), :].astype(bf16)


def costs(qall, kp_ref, cost_ref):
    @pl.loop(0, NK // 512)
    def _(jj):
        for u in range(2):
            j = jj * 2 + u
            o = dot_nt(qall[...], kp_ref[pl.ds(pl.multiple_of(j * 256, 256), 256), :])
            for v in range(NQ // 4):
                for h in range(2):
                    cost_ref[pl.ds(v * 256 + (j * 2 + h) * 4, 4), :] = o[v * 4 : v * 4 + 4, h * 128 : (h + 1) * 128]


def pipeline(mask_ref, wd_ref, bias_ref, gain_ref, smap_ref, w_ref, lse_ref, cost_ref, toks, nrms, ps, ms, after):
    lane = lax.broadcasted_iota(jnp.int32, (8, 128), 1)
    sub = lax.broadcasted_iota(jnp.int32, (8, 128), 0)
    lane64 = lax.broadcasted_iota(jnp.int32, (64, 128), 1)

    def sums(g, slot):
        nrm_ref, p_ref, m_ref = nrms[slot], ps[slot], ms[slot]
        b2 = lax.rem(g + 1, 2) * 2
        zero = jnp.zeros((16, 128), bf16)
        rows = []
        for lp in range(LAT):
            st = jnp.bitwise_xor(b2, lp)
            pa = p_ref[pl.ds(st, 16, stride=8), :].astype(bf16)
            pb = p_ref[pl.ds(st + 128, 16, stride=8), :].astype(bf16)
            rows += [jnp.concatenate([pa, zero], axis=1), jnp.concatenate([zero, pb], axis=1)]
        pst = jnp.concatenate(rows, axis=0)
        acc = None
        for k in range(NP // 4):
            o = dot_nt(nrm_ref[k * 256 : (k + 1) * 256, :], pst)
            for i in range(4):
                ov = [o[i * 64 : (i + 1) * 64, v * 128 : (v + 1) * 128] for v in range(2)]
                own = lax.bitwise_and(lane64, 15) == k * 4 + i
                acc = ov if acc is None else [jnp.where(own, ov[v], acc[v]) for v in range(2)]
            if k < NP // 4 - 1:
                yield
        d = dot_nt(jnp.ones((16, 256), bf16), pst)[0:1, :]
        rd = 1.0 / d
        for v in range(2):
            vl = slice(v * 128, (v + 1) * 128)
            w_ref[pl.ds(pl.multiple_of(g * 64, 64), 64), vl] = acc[v] * rd[:, vl]
        lse_ref[pl.ds(pl.multiple_of(g * 8, 8), 8), :] = jnp.broadcast_to(m_ref[0:1, :] + jnp.log(d), (8, 256))
        yield

    def scores(g, slot):
        nrm_ref, p_ref, m_ref = nrms[slot], ps[slot], ms[slot]
        b2 = lax.rem(g, 2) * 2
        pos = lane - lax.bitwise_and(jnp.bitwise_xor(sub, b2), 3) * 32
        accm = jnp.zeros((8, 128), f32)
        for k in range(NP // 4):
            s3 = jnp.dot(smap_ref[...], nrm_ref[k * 256 : (k + 1) * 256, :], preferred_element_type=f32)
            for i in range(4):
                s = s3[24 * i : 24 * i + 8] + (s3[24 * i + 8 : 24 * i + 16] + s3[24 * i + 16 : 24 * i + 24])
                for h in range(2):
                    q = h * 16 + k * 4 + i
                    sq = s[:, h * 128 : (h + 1) * 128]
                    m = jnp.broadcast_to(jnp.max(sq, axis=1, keepdims=True), (8, 128))
                    p_ref[q * 8 : q * 8 + 8, :] = jnp.exp(sq - m)
                    accm = jnp.where(pos == q, m, accm)
            if k < NP // 4 - 1:
                yield
        m_ref[:, 0:128] = jnp.broadcast_to(jnp.sum(jnp.where(sub < 4, accm, 0.0), axis=0, keepdims=True), (8, 128))
        m_ref[:, 128:256] = jnp.broadcast_to(jnp.sum(jnp.where(sub < 4, 0.0, accm), axis=0, keepdims=True), (8, 128))
        yield

    def norms(slot):
        tok_ref, nrm_ref = toks[slot], nrms[slot]
        for i in range(NP):
            for h in range(2):
                hl = slice(h * 128, (h + 1) * 128)
                tok = tok_ref[i * 64 : (i + 1) * 64, hl] + bias_ref[:, hl]
                ss = jnp.sum(tok * tok, axis=0, keepdims=True)
                rstd = lax.rsqrt(ss * (1.0 / E) + 1e-5)
                nrm_ref[i * 64 : (i + 1) * 64, hl] = (tok * rstd * gain_ref[:, hl]).astype(bf16)
                yield

    def tokens(g, slot):
        q0 = jnp.minimum(g, NG - 1) * G
        for k in range(NP // 2):
            rows = []
            for i in range(2):
                xs = []
                for h in range(2):
                    q = h * 16 + k * 2 + i
                    base = pl.multiple_of((q0 + q // 4 * 4) * CELLS, 256) + q % 4
                    xq = cost_ref[pl.ds(base, CELLS, stride=4), :].astype(bf16)
                    mk = jnp.broadcast_to(mask_ref[pl.ds(q0 + q, 1), :].astype(f32), (CELLS, NT)).astype(bf16)
                    xs.append(xq * mk)
                xx = jnp.concatenate(xs, axis=1)
                rows += [xx, xx]
            toks[slot][k * 128 : (k + 1) * 128, :] = jnp.dot(
                wd_ref[...], jnp.concatenate(rows, axis=0), preferred_element_type=f32
            )
            yield

    @pl.loop(0, (NG + 3 + 2) // 3)
    def _(it):
        for u in range(3):
            g = it * 3 + u

            @pl.when(g < NG + 3)
            def _():
                steps = {
                    "w": sums(g, u), "s": scores(g, (u + 1) % 3), "n": norms((u + 2) % 3), "t": tokens(g, u),
                }
                for step in "snn" * 4 + "wnnnn" * 4 + "tn" * 8:
                    next(steps[step])
                after(g)


def split(a, n):
    parts = []
    for _ in range(n):
        parts.append(a.astype(bf16).astype(f32))
        a = a - parts[-1]
    return parts


def parameters(weight_ref, pbias_ref, pgain_ref, latq_ref, key_ref, wd_ref, bias_ref, gain_ref, smap_ref):
    weight = weight_ref[...].astype(f32).T
    centred = (weight - jnp.mean(weight, axis=0, keepdims=True)) / math.sqrt(CH)
    parts = jnp.concatenate(split(centred, 2), axis=1)
    zero = jnp.zeros((E, 128), f32)
    wd_ref[...] = jnp.concatenate(
        [jnp.concatenate([parts, zero], axis=1), jnp.concatenate([zero, parts], axis=1)], axis=0
    ).astype(bf16)
    bias = pbias_ref[...]
    bias = bias - jnp.mean(bias, axis=1, keepdims=True)
    for source, ref in ((bias, bias_ref), (pgain_ref[...], gain_ref)):
        column = jnp.broadcast_to(source, (128, E)).T
        ref[:, 0:128] = column
        ref[:, 128:256] = column
    score_map = lax.dot_general(
        latq_ref[...], key_ref[...].astype(f32), (((1,), (1,)), ((), ())),
        precision=lax.Precision.HIGHEST, preferred_element_type=f32,
    ) / math.sqrt(LD)
    parts = jnp.concatenate(split(score_map, 3), axis=0)
    zero = jnp.zeros_like(parts)
    smap_ref[...] = jnp.concatenate(
        [jnp.concatenate([parts if i == j else zero for j in range(4)], axis=1) for i in range(4)], axis=0
    ).astype(bf16)


def kernel(
    q_ref, k_ref, mask_ref, weight_ref, pbias_ref, pgain_ref, latq_ref, key_ref, value_ref, out_ref,
    kbuf, qbuf, kf_ref, kp_ref, qall, cost_ref, toks, nrms, ps, ms, w_ref, lse_ref, wd_ref, bias_ref, gain_ref, smap_ref,
    sbuf, sst, rbuf, rst, ssem, rsem, qssem, qrsem, dssem, drsem, tssem, trsem,
):
    me = lax.axis_index("pb")
    y = lax.axis_index("ka")
    def prepare():
        parameters(weight_ref, pbias_ref, pgain_ref, latq_ref, key_ref, wd_ref, bias_ref, gain_ref, smap_ref)
        for refs in (ps, ms, nrms, toks):
            for ref in refs:
                ref[...] = jnp.ones_like(ref)

    gather(me, y, k_ref, q_ref, kbuf, qbuf, ssem, rsem, qssem, qrsem, prepare)
    qall[...] = jnp.concatenate([qbuf[i] for i in range(NY)], axis=0).astype(f32).T.astype(bf16)
    order_keys(kbuf, kf_ref, kp_ref)
    costs(qall, kp_ref, cost_ref)
    lane64 = lax.broadcasted_iota(jnp.int32, (64, 128), 1)
    lane8 = lax.broadcasted_iota(jnp.int32, (8, 128), 1)

    def copies(k, o):
        to = lax.rem(y + o, NY)
        rows = pl.ds(pl.multiple_of(k * 128, 128), 128)
        st = pl.ds(pl.multiple_of(k * 16, 16), 16)
        return (
            pltpu.make_async_remote_copy(
                src_ref=sbuf.at[to, rows], dst_ref=rbuf.at[o - 1, rows], send_sem=dssem.at[o - 1, k],
                recv_sem=drsem.at[o - 1, k], device_id=(me, to), device_id_type=MESH,
            ),
            pltpu.make_async_remote_copy(
                src_ref=sst.at[to, st], dst_ref=rst.at[o - 1, st], send_sem=tssem.at[o - 1, k],
                recv_sem=trsem.at[o - 1, k], device_id=(me, to), device_id_type=MESH,
            ),
        )

    def send_chunk(k):
        for blk in range(2):
            ga = k * GPC + blk * 2 + 3
            for v in range(2):
                vl = slice(v * 128, (v + 1) * 128)
                wa = w_ref[pl.ds(pl.multiple_of(ga * 64, 64), 64), vl]
                wb = w_ref[pl.ds(pl.multiple_of(ga * 64 + 64, 64), 64), vl]
                la = lse_ref[pl.ds(pl.multiple_of(ga * 8, 8), 8), vl]
                lb = lse_ref[pl.ds(pl.multiple_of(ga * 8 + 8, 8), 8), vl]
                rows = pl.ds(pl.multiple_of(k * 128 + blk * 64, 64), 64)
                st = pl.ds(pl.multiple_of(k * 16 + blk * 8, 8), 8)
                sbuf[2 * v, rows, :] = jnp.where(lane64 < 64, wa, wb).astype(bf16)
                sbuf[2 * v + 1, rows, :] = jnp.where(lane64 < 64, wb, wa).astype(bf16)
                sst[2 * v, st, :] = jnp.where(lane8 < 64, la, lb)
                sst[2 * v + 1, st, :] = jnp.where(lane8 < 64, lb, la)
        for o in range(1, NY):
            for c in copies(k, o):
                c.start()

    def combine_chunk(k):
        for o in range(1, NY):
            for c in copies(k, o):
                c.wait_recv()
        odd = lax.rem(y, 2)
        for blk in range(2):
            rows = pl.ds(pl.multiple_of(k * 128 + blk * 64, 64), 64)
            st = pl.ds(pl.multiple_of(k * 16 + blk * 8, 8), 8)
            lses = [sst[y, st, :]] + [rst[o, st, :] for o in range(NY - 1)]
            vals = [sbuf[y, rows, :]] + [rbuf[o, rows, :] for o in range(NY - 1)]
            top = jnp.maximum(jnp.maximum(lses[0], lses[1]), jnp.maximum(lses[2], lses[3]))
            facs = [jnp.exp(a - top) for a in lses]
            inv = 1.0 / (facs[0] + facs[1] + facs[2] + facs[3])
            pooled = sum(v.astype(f32) * (a * inv)[0:1, :] for v, a in zip(vals, facs))
            res = lax.dot_general(
                pooled.astype(bf16), value_ref[...], (((0,), (0,)), ((), ())), preferred_element_type=f32
            ).astype(bf16)
            for half in range(2):
                off = odd * 32 if half == 0 else (1 - odd) * 32
                orow = pl.ds(pl.multiple_of(k * 128 + blk * 64 + off, 32), 32)
                for l in range(2):
                    r = (half * 2 + l) * 32
                    out_ref[orow, l * 128 : (l + 1) * 128] = res[r : r + 32, :]

    def after(g):
        @pl.when(jnp.logical_and(lax.rem(g, GPC) == 2, g > 3))
        def _():
            k = lax.div(g - 3, GPC)
            send_chunk(k)

            @pl.when(k > 0)
            def _():
                combine_chunk(k - 1)

    pipeline(mask_ref, wd_ref, bias_ref, gain_ref, smap_ref, w_ref, lse_ref, cost_ref, toks, nrms, ps, ms, after)
    combine_chunk(NCH - 1)

    @pl.loop(0, NCH)
    def _(k):
        for o in range(1, NY):
            for c in copies(k, o):
                c.wait_send()


def body(
    query_features, key_features, patch_weight, patch_bias, norm_gain, latent_queries, key_weight, value_weight, keep_mask
):
    vmem = pl.BlockSpec(memory_space=pltpu.VMEM)
    dma = pltpu.SemaphoreType.DMA
    out = pl.pallas_call(
        kernel,
        out_shape=jax.ShapeDtypeStruct((NQ, 2 * LD), bf16),
        in_specs=[vmem] * 9,
        out_specs=vmem,
        scratch_shapes=[
            pltpu.VMEM((2 * NX * NZ, 128, CH), bf16),
            pltpu.VMEM((NY, CH // NY, NQ), bf16),
            pltpu.VMEM((2 * NK, 128), f32),
            pltpu.VMEM((NK, CH), bf16),
            pltpu.VMEM((NQ, CH), bf16),
            pltpu.VMEM((CELLS * NQ, NT), f32),
            [pltpu.VMEM((NP * E, 256), f32)] * 3,
            [pltpu.VMEM((NP * E, 256), bf16)] * 3,
            [pltpu.VMEM((G * LAT, NT), f32)] * 3,
            [pltpu.VMEM((8, 256), f32)] * 3,
            pltpu.VMEM(((NG + 3) * E, 256), f32),
            pltpu.VMEM(((NG + 3) * 8, 256), f32),
            pltpu.VMEM((2 * E, 256), bf16),
            pltpu.VMEM((E, 256), f32),
            pltpu.VMEM((E, 256), f32),
            pltpu.VMEM((96, 256), bf16),
            pltpu.VMEM((NY, NQ, 128), bf16),
            pltpu.VMEM((NY, NCH * 16, 128), f32),
            pltpu.VMEM((NY - 1, NQ, 128), bf16),
            pltpu.VMEM((NY - 1, NCH * 16, 128), f32),
            dma((64,)),
            dma((64,)),
            dma((NY - 1,)),
            dma((NY - 1,)),
            dma((NY - 1, NCH)),
            dma((NY - 1, NCH)),
            dma((NY - 1, NCH)),
            dma((NY - 1, NCH)),
        ],
        compiler_params=pltpu.CompilerParams(
            collective_id=0, has_side_effects=True, vmem_limit_bytes=60 * 1024 * 1024
        ),
    )(
        query_features.T, key_features, keep_mask, patch_weight, patch_bias.reshape(1, E), norm_gain.reshape(1, E),
        latent_queries, key_weight, value_weight,
    )
    return out.reshape(NQ, 2, LD)


def solution(mesh):
    placed = (P("pb", "ka"), P(("ka", "pb"), None), P(), P(), P(), P(), P(), P(), P("pb", "ka"))
    return jax.shard_map(
        body, mesh=mesh, in_specs=placed, out_specs=P("pb", "ka", None), check_vma=False
    )
```

time: 327 us -> 79.7 us (0.24)
  waiting for transfers between devices: 110 us -> 0 us
  Pallas kernels: 0 us -> 77.4 us
  matrix products: 76.4 us -> 0 us
  local copies, waits for them, and re-layouts: 58 us -> 1.78 us
  other arithmetic: 34.4 us -> 0 us
  blocking collectives: 31.7 us -> 0 us
  between operations: 13.5 us -> 0.01 us
    all_gather x2 -> x0, waiting for transfers between devices: 110 us -> none  [the longest x1 72.3 us: body(): key_block = lax.all_gather(key_features, 'pb', axis=0, tiled=True)]
    pallas_call x0 -> x1, Pallas kernels: none -> 77.4 us  [body(): pl.pallas_call(kernel, out_shape=jax.ShapeDtypeStruct((NQ, 2 * LD), bf16)...]
    dot_general x42 -> x0, matrix products: 76.4 us -> none  [the longest x10 35.6 us: one_block(): lax.dot_general(query_rows, key_block, (((1,), (1,)), ((), ())), preferre...]
    all_gather x3 -> x0, blocking collectives: 31.7 us -> none  [the longest x2 19.7 us: joined(): gathered = jax.tree.map(lambda a: lax.all_gather(a, axis), part)]
    dot_general x10 -> x0, local copies, waits for them, and re-layouts: 22.9 us -> none  [one_block(): jnp.dot(cost_tile, patch_weight, preferred_element_type=jnp.float32)]
    dynamic_slice x7 -> x0, local copies, waits for them, and re-layouts: 14.7 us -> none  [the longest x6 14.7 us: take(): lax.dynamic_index_in_dim(a, source, 0, False)]
    add x6 -> x0, other arithmetic: 14.5 us -> none  [the longest x3 14.5 us: combine_parts(): val_first * fac_first[:, :, None] + val_second * fac_second[:, :, None]]
    convert_element_type x20 -> x0, other arithmetic: 12.9 us -> none  [the longest x10 7.61 us: one_block(): tokens = tokens * mask_rows[:, :, None].astype(jnp.float32) + patch_bias]
  transfers between devices with their start and end apart: 2 -> 0, of which waited for: 2 -> 0; matrix products, arithmetic and copies ran while one was open for 1% -> 0% of each run, Pallas kernels for 0% -> 0%
where the time goes in v1:
time: 79.7 us; the launch traced here: 79.2 us
  Pallas kernels  77.4 us (97%)
  local copies, waits for them, and re-layouts  1.78 us (2%)
    pallas_call x1, Pallas kernels, body(): pl.pallas_call(kernel, out_shape=jax.ShapeDtypeStruct((NQ, 2 * LD), bf16)...  77.4 us
    reshape x1, local copies, waits for them, and re-layouts, body(): return out.reshape(NQ, 2, LD)  1.78 us

profile of v1, /device:TPU:1, one launch (start us, length us, event | category | flops | bytes accessed | tf_op | source)
XLA Modules:
  0.0 79.2 jit_solution(2640709323484532669)
XLA Ops:
  0.0 77.4 %shard_map.91 = bf16[640,256]{1,0:T(8,128)(2,1)} custom-call(bf16[64,640]{1,0:T(8,128)(2,1)} %bitcast.3, bf16[128,256]{1,0:T(8,128)(2,1)} %k_ref.1, s32[640,128]{1,0:T(8,128)} %mask_ref.1, bf16[64,64]{1,0:T(8,128)(2,1)} %weight_ref.1, f32[1,64]{1,0:T(1,128)} %bitcast.4, f32[1,64]{1,0:T(1,128)} %bitcast.5, f32[8,128]{1,0:T(8,128)} %latq_ref.1, ...), custom_call_target="tpu_custom_call" | custom-call | tf_op jit(solution)/shard_map/pallas_call | solution.py:405
  77.4 1.8 %reshape.11 = bf16[640,2,128]{2,1,0:T(2,128)(2,1)} reshape(bf16[640,256]{1,0:T(8,128)(2,1)} %shard_map.91) | data formatting | bytes 655360 | tf_op jit(solution)/shard_map/reshape | solution.py:447

commit v2 on v1

--- a/solution.py
+++ b/solution.py
@@ -26,7 +26,7 @@
     return lax.dot_general(a, b, (((1,), (1,)), ((), ())), preferred_element_type=f32)
 
 
-def gather(me, y, k_ref, q_ref, kbuf, qbuf, ssem, rsem, qssem, qrsem, prepare):
+def gather(me, y, k_ref, q_ref, kbuf, qbuf, ssem, rsem, qssem, qrsem, prepare, queries):
     core = lax.rem(me, 2)
     z = lax.rem(lax.div(me, 2), NZ)
     x = lax.div(me, 2 * NZ)
@@ -35,8 +35,8 @@
         return (lax.rem(xx + NX, NX) * NZ + lax.rem(zz + NZ, NZ)) * 2 + cc
 
     sibling = pb(x, z, 1 - core)
-    ring = {"z+": pb(x, z + 1, core), "z-": pb(x, z - 1, core), "x+": pb(x + 1, z, core), "x-": pb(x - 1, z, core)}
-    ring["s"] = sibling
+    ring = {f"z{d}": pb(x, z + d, core) for d in range(1, NZ)}
+    ring.update({"x+": pb(x + 1, z, core), "x-": pb(x - 1, z, core), "x2": pb(x + 2, z, core), "s": sibling})
 
     barrier = pltpu.get_barrier_semaphore()
     for other in ring.values():
@@ -75,49 +75,42 @@
         return count[0]
 
     def z_first(send, arrive):
-        zs = [(z, None, 0), (z - 1, "z+", 1), (z + 1, "z-", 1), (z - 2, "z+", 2), (z + 2, "z-", 2), (z - 3, "z+", 3), (z + 3, "z-", 3), (z - 4, "z+", 4)]
-        send(me, "z+", "z-", "x+", "x-", "s")
-        for k in range(1, NZ + 2):
-            if k < NZ:
-                zz, way, dist = zs[k]
-                slot = pb(x, zz, core)
-                arrive(slot)
-                if dist < (4 if way == "z+" else 3):
-                    send(slot, way)
-                send(slot, "x+", "x-", "s")
-            if k <= NZ:
-                i = k - 1
-                slot = pb(x - 1, zs[i][0], core)
-                arrive(slot)
-                send(slot, *(("x+", "s") if i % 2 == 0 else ("s",)))
-                slot = pb(x + 1, zs[i][0], core)
-                arrive(slot)
-                send(slot, *(("x-", "s") if i % 2 == 1 else ("s",)))
-            if k >= 2:
-                slot = pb(x + 2, zs[k - 2][0], core)
-                arrive(slot)
-                send(slot, "s")
+        zs = [z, z - 1, z + 1, z - 2, z + 2, z - 3, z + 3, z - 4]
+        send(me, *(f"z{d}" for d in (1, 7, 2, 6, 3, 5, 4)), "x+", "x-", "s")
+        for zz in zs[1:]:
+            slot = pb(x, zz, core)
+            arrive(slot)
+            send(slot, "x+", "x-", "s")
+        for i, zz in enumerate(zs):
+            slot = pb(x - 1, zz, core)
+            arrive(slot)
+            send(slot, *(("x+", "s") if i % 2 == 0 else ("s",)))
+            slot = pb(x + 1, zz, core)
+            arrive(slot)
+            send(slot, *(("x-", "s") if i % 2 == 1 else ("s",)))
+        for zz in zs:
+            slot = pb(x + 2, zz, core)
+            arrive(slot)
+            send(slot, "s")
 
     def x_first(send, arrive):
-        send(me, "z+", "z-", "x+", "x-", "s")
+        send(me, "z1", "z7", "x+", "x-", "x2", "s")
         xs = [x, x - 1, x + 1, x + 2]
         for i in range(1, NX):
             slot = pb(xs[i], z, core)
             arrive(slot)
-            if i == 1:
-                send(slot, "x+")
-            send(slot, "z+", "z-", "s")
+            send(slot, "z1", "z7", "s")
         for dist in range(1, 5):
             for i in range(NX):
                 last_plus, last_minus = (4, 3) if i < 2 else (3, 4)
                 if dist <= last_plus:
                     slot = pb(xs[i], z - dist, core)
                     arrive(slot)
-                    send(slot, *(("z+", "s") if dist < last_plus else ("s",)))
+                    send(slot, *(("z1", "s") if dist < last_plus else ("s",)))
                 if dist <= last_minus:
                     slot = pb(xs[i], z + dist, core)
                     arrive(slot)
-                    send(slot, *(("z-", "s") if dist < last_minus else ("s",)))
+                    send(slot, *(("z7", "s") if dist < last_minus else ("s",)))
 
     for o in range(1, NY):
         q_copy(o).start()
@@ -130,13 +123,14 @@
     def _():
         assert run(x_first) == 63
 
+    for o in range(1, NY):
+        q_copy(o).wait()
+    queries()
+
     @pl.loop(0, NX * NZ)
     def _(i):
         copy(2 * i + 1 - core, sibling, 0).wait_recv()
 
-    for o in range(1, NY):
-        q_copy(o).wait()
-
     @pl.loop(0, 63)
     def _(i):
         copy(me, sibling, i).wait_send()
@@ -145,26 +139,39 @@
 def order_keys(kbuf, kf_ref, kp_ref):
     @pl.loop(0, NX * NZ * 2)
     def _(s):
-        r = pl.multiple_of(s * 128, 128)
-        for h in range(2):
-            kf_ref[pl.ds(r + h * NK, 128), :] = kbuf[s, :, h * 128 : (h + 1) * 128].astype(f32)
-
-    @pl.loop(0, CELLS)
-    def _(c):
-        for h in range(2):
-            rows = pl.ds(pl.multiple_of(c * NT, NT), NT)
-            kp_ref[rows, h * 128 : (h + 1) * 128] = kf_ref[pl.ds(c + h * NK, NT, stride=CELLS), :].astype(bf16)
+        for i in range(2):
+            base = lax.div(s, 4) * 512 + (lax.rem(s, 4) * 2 + i) * 8
+            for c in range(CELLS // 8):
+                for h in range(2):
+                    to = pl.multiple_of(base + c * 64, 8) + h * NK
+                    kf_ref[pl.ds(to, 8), :] = kbuf[s, i * CELLS + c * 8 : i * CELLS + c * 8 + 8, h * 128 : (h + 1) * 128].astype(f32)
+
+    @pl.loop(0, CELLS // 4)
+    def _(i):
+        for u in range(4):
+            base = pl.multiple_of(lax.div(i, 2) * 64, 64) + lax.rem(i, 2) * 4 + u
+            for h in range(2):
+                for t in range(0, NT // 8, 2):
+                    pair = [kf_ref[pl.ds(base + (t + j) * 512 + h * NK, 8, stride=8), :] for j in range(2)]
+                    rows = pl.ds(pl.multiple_of((i * 4 + (0, 2, 1, 3)[u]) * NT + t * 8, 16), 16)
+                    kp_ref[rows, h * 128 : (h + 1) * 128] = jnp.concatenate(pair, axis=0).astype(bf16)
 
 
 def costs(qall, kp_ref, cost_ref):
-    @pl.loop(0, NK // 512)
-    def _(jj):
-        for u in range(2):
-            j = jj * 2 + u
-            o = dot_nt(qall[...], kp_ref[pl.ds(pl.multiple_of(j * 256, 256), 256), :])
-            for v in range(NQ // 4):
-                for h in range(2):
-                    cost_ref[pl.ds(v * 256 + (j * 2 + h) * 4, 4), :] = o[v * 4 : v * 4 + 4, h * 128 : (h + 1) * 128]
+    low = lax.broadcasted_iota(jnp.int32, (8, 128), 0) < 4
+
+    @pl.loop(0, CELLS // 4)
+    def _(j):
+        r = pl.multiple_of(j * 512, 512)
+        even = dot_nt(qall[0], kp_ref[pl.ds(r, 256), :])
+        odd = dot_nt(qall[1], kp_ref[pl.ds(r + 256, 256), :])
+        for v in range(NQ // 8):
+            for h in range(2):
+                ev = even[v * 8 : v * 8 + 8, h * 128 : (h + 1) * 128]
+                od = odd[v * 8 : v * 8 + 8, h * 128 : (h + 1) * 128]
+                to = pl.multiple_of(v * 512 + j * 16 + h * 8, 8)
+                cost_ref[pl.ds(to, 8), :] = jnp.where(low, ev, od)
+                cost_ref[pl.ds(to + 256, 8), :] = jnp.where(low, od, ev)
 
 
 def pipeline(mask_ref, wd_ref, bias_ref, gain_ref, smap_ref, w_ref, lse_ref, cost_ref, toks, nrms, ps, ms, after):
@@ -183,16 +190,13 @@
             pb = p_ref[pl.ds(st + 128, 16, stride=8), :].astype(bf16)
             rows += [jnp.concatenate([pa, zero], axis=1), jnp.concatenate([zero, pb], axis=1)]
         pst = jnp.concatenate(rows, axis=0)
+        o = dot_nt(jnp.concatenate([nrm_ref[...], jnp.ones((16, 256), bf16)], axis=0), pst)
         acc = None
-        for k in range(NP // 4):
-            o = dot_nt(nrm_ref[k * 256 : (k + 1) * 256, :], pst)
-            for i in range(4):
-                ov = [o[i * 64 : (i + 1) * 64, v * 128 : (v + 1) * 128] for v in range(2)]
-                own = lax.bitwise_and(lane64, 15) == k * 4 + i
-                acc = ov if acc is None else [jnp.where(own, ov[v], acc[v]) for v in range(2)]
-            if k < NP // 4 - 1:
-                yield
-        d = dot_nt(jnp.ones((16, 256), bf16), pst)[0:1, :]
+        for p in range(NP):
+            ov = [o[p * 64 : (p + 1) * 64, v * 128 : (v + 1) * 128] for v in range(2)]
+            own = lax.bitwise_and(lane64, 15) == p
+            acc = ov if acc is None else [jnp.where(own, ov[v], acc[v]) for v in range(2)]
+        d = o[NP * 64 : NP * 64 + 1, :]
         rd = 1.0 / d
         for v in range(2):
             vl = slice(v * 128, (v + 1) * 128)
@@ -247,7 +251,7 @@
                 xx = jnp.concatenate(xs, axis=1)
                 rows += [xx, xx]
             toks[slot][k * 128 : (k + 1) * 128, :] = jnp.dot(
-                wd_ref[...], jnp.concatenate(rows, axis=0), preferred_element_type=f32
+                wd_ref[k % 4 // 2], jnp.concatenate(rows, axis=0), preferred_element_type=f32
             )
             yield
 
@@ -261,7 +265,7 @@
                 steps = {
                     "w": sums(g, u), "s": scores(g, (u + 1) % 3), "n": norms((u + 2) % 3), "t": tokens(g, u),
                 }
-                for step in "snn" * 4 + "wnnnn" * 4 + "tn" * 8:
+                for step in "w" + "n" * 16 + "snn" * 4 + "tn" * 8:
                     next(steps[step])
                 after(g)
 
@@ -275,13 +279,17 @@
 
 
 def parameters(weight_ref, pbias_ref, pgain_ref, latq_ref, key_ref, wd_ref, bias_ref, gain_ref, smap_ref):
-    weight = weight_ref[...].astype(f32).T
-    centred = (weight - jnp.mean(weight, axis=0, keepdims=True)) / math.sqrt(CH)
-    parts = jnp.concatenate(split(centred, 2), axis=1)
+    weight = weight_ref[...].astype(f32)
+    even = lax.rem(lax.broadcasted_iota(jnp.int32, (CELLS, E), 0), 2) == 0
+    swapped = jnp.where(even, pltpu.roll(weight, CELLS - 1, 0), pltpu.roll(weight, 1, 0))
     zero = jnp.zeros((E, 128), f32)
-    wd_ref[...] = jnp.concatenate(
-        [jnp.concatenate([parts, zero], axis=1), jnp.concatenate([zero, parts], axis=1)], axis=0
-    ).astype(bf16)
+    for i, form in enumerate((weight, swapped)):
+        form = form.T
+        centred = (form - jnp.mean(form, axis=0, keepdims=True)) / math.sqrt(CH)
+        parts = jnp.concatenate(split(centred, 2), axis=1)
+        wd_ref[i] = jnp.concatenate(
+            [jnp.concatenate([parts, zero], axis=1), jnp.concatenate([zero, parts], axis=1)], axis=0
+        ).astype(bf16)
     bias = pbias_ref[...]
     bias = bias - jnp.mean(bias, axis=1, keepdims=True)
     for source, ref in ((bias, bias_ref), (pgain_ref[...], gain_ref)):
@@ -312,8 +320,12 @@
             for ref in refs:
                 ref[...] = jnp.ones_like(ref)
 
-    gather(me, y, k_ref, q_ref, kbuf, qbuf, ssem, rsem, qssem, qrsem, prepare)
-    qall[...] = jnp.concatenate([qbuf[i] for i in range(NY)], axis=0).astype(f32).T.astype(bf16)
+    def queries():
+        rows = jnp.concatenate([qbuf[i] for i in range(NY)], axis=0).astype(f32).T
+        qall[0] = rows.astype(bf16)
+        qall[1] = pltpu.roll(rows.reshape(NQ // 8, 8, CH), 4, 1).reshape(NQ, CH).astype(bf16)
+
+    gather(me, y, k_ref, q_ref, kbuf, qbuf, ssem, rsem, qssem, qrsem, prepare, queries)
     order_keys(kbuf, kf_ref, kp_ref)
     costs(qall, kp_ref, cost_ref)
     lane64 = lax.broadcasted_iota(jnp.int32, (64, 128), 1)
@@ -383,12 +395,11 @@
             k = lax.div(g - 3, GPC)
             send_chunk(k)
 
-            @pl.when(k > 0)
-            def _():
-                combine_chunk(k - 1)
-
     pipeline(mask_ref, wd_ref, bias_ref, gain_ref, smap_ref, w_ref, lse_ref, cost_ref, toks, nrms, ps, ms, after)
-    combine_chunk(NCH - 1)
+
+    @pl.loop(0, NCH)
+    def _(k):
+        combine_chunk(k)
 
     @pl.loop(0, NCH)
     def _(k):
@@ -412,7 +423,7 @@
             pltpu.VMEM((NY, CH // NY, NQ), bf16),
             pltpu.VMEM((2 * NK, 128), f32),
             pltpu.VMEM((NK, CH), bf16),
-            pltpu.VMEM((NQ, CH), bf16),
+            pltpu.VMEM((2, NQ, CH), bf16),
             pltpu.VMEM((CELLS * NQ, NT), f32),
             [pltpu.VMEM((NP * E, 256), f32)] * 3,
             [pltpu.VMEM((NP * E, 256), bf16)] * 3,
@@ -420,7 +431,7 @@
             [pltpu.VMEM((8, 256), f32)] * 3,
             pltpu.VMEM(((NG + 3) * E, 256), f32),
             pltpu.VMEM(((NG + 3) * 8, 256), f32),
-            pltpu.VMEM((2 * E, 256), bf16),
+            pltpu.VMEM((2, 2 * E, 256), bf16),
             pltpu.VMEM((E, 256), f32),
             pltpu.VMEM((E, 256), f32),
             pltpu.VMEM((96, 256), bf16),

time: 79.7 us -> 63.6 us (0.80)
  Pallas kernels: 77.4 us -> 61.7 us
    pallas_call x1, Pallas kernels: 77.4 us -> 61.7 us  [body(): pl.pallas_call(kernel, out_shape=jax.ShapeDtypeStruct((NQ, 2 * LD), bf16)...]
where the time goes in v2:
time: 63.6 us; the launch traced here: 63.5 us
  Pallas kernels  61.7 us (97%)
  local copies, waits for them, and re-layouts  1.78 us (3%)
    pallas_call x1, Pallas kernels, body(): pl.pallas_call(kernel, out_shape=jax.ShapeDtypeStruct((NQ, 2 * LD), bf16)...  61.7 us
    reshape x1, local copies, waits for them, and re-layouts, body(): return out.reshape(NQ, 2, LD)  1.78 us

profile of v2, /device:TPU:1, one launch (start us, length us, event | category | flops | bytes accessed | tf_op | source)
XLA Modules:
  0.0 63.5 jit_solution(9954857854155178427)
XLA Ops:
  0.0 61.7 %shard_map.91 = bf16[640,256]{1,0:T(8,128)(2,1)} custom-call(bf16[64,640]{1,0:T(8,128)(2,1)} %bitcast.3, bf16[128,256]{1,0:T(8,128)(2,1)} %k_ref.1, s32[640,128]{1,0:T(8,128)} %mask_ref.1, bf16[64,64]{1,0:T(8,128)(2,1)} %weight_ref.1, f32[1,64]{1,0:T(1,128)} %bitcast.4, f32[1,64]{1,0:T(1,128)} %bitcast.5, f32[8,128]{1,0:T(8,128)} %latq_ref.1, ...), custom_call_target="tpu_custom_call" | custom-call | tf_op jit(solution)/shard_map/pallas_call | solution.py:416
  61.7 1.8 %reshape.11 = bf16[640,2,128]{2,1,0:T(2,128)(2,1)} reshape(bf16[640,256]{1,0:T(8,128)(2,1)} %shard_map.91) | data formatting | bytes 655360 | tf_op jit(solution)/shard_map/reshape | solution.py:458

commit v3 on v2

--- a/solution.py
+++ b/solution.py
@@ -26,7 +26,7 @@
     return lax.dot_general(a, b, (((1,), (1,)), ((), ())), preferred_element_type=f32)
 
 
-def gather(me, y, k_ref, q_ref, kbuf, qbuf, ssem, rsem, qssem, qrsem, prepare, queries):
+def gather(me, y, k_ref, q_ref, kbuf, qbuf, ssem, rsem, qssem, qrsem, prepare, queries, landed):
     core = lax.rem(me, 2)
     z = lax.rem(lax.div(me, 2), NZ)
     x = lax.div(me, 2 * NZ)
@@ -67,6 +67,7 @@
             for way in ways:
                 copy(slot, ring[way], count[0]).start()
                 count[0] += 1
+            landed(slot)
 
         def arrive(slot):
             copy(slot, sibling, 0).wait_recv()
@@ -130,22 +131,23 @@
     @pl.loop(0, NX * NZ)
     def _(i):
         copy(2 * i + 1 - core, sibling, 0).wait_recv()
+        landed(2 * i + 1 - core)
 
     @pl.loop(0, 63)
     def _(i):
         copy(me, sibling, i).wait_send()
 
 
-def order_keys(kbuf, kf_ref, kp_ref):
-    @pl.loop(0, NX * NZ * 2)
-    def _(s):
-        for i in range(2):
-            base = lax.div(s, 4) * 512 + (lax.rem(s, 4) * 2 + i) * 8
-            for c in range(CELLS // 8):
-                for h in range(2):
-                    to = pl.multiple_of(base + c * 64, 8) + h * NK
-                    kf_ref[pl.ds(to, 8), :] = kbuf[s, i * CELLS + c * 8 : i * CELLS + c * 8 + 8, h * 128 : (h + 1) * 128].astype(f32)
-
+def spread(slot, kbuf, kf_ref):
+    for i in range(2):
+        base = lax.div(slot, 4) * 512 + (lax.rem(slot, 4) * 2 + i) * 8
+        for c in range(CELLS // 8):
+            for h in range(2):
+                to = pl.multiple_of(base + c * 64, 8) + h * NK
+                kf_ref[pl.ds(to, 8), :] = kbuf[slot, i * CELLS + c * 8 : i * CELLS + c * 8 + 8, h * 128 : (h + 1) * 128].astype(f32)
+
+
+def order_keys(kf_ref, kp_ref):
     @pl.loop(0, CELLS // 4)
     def _(i):
         for u in range(4):
@@ -160,18 +162,20 @@
 def costs(qall, kp_ref, cost_ref):
     low = lax.broadcasted_iota(jnp.int32, (8, 128), 0) < 4
 
-    @pl.loop(0, CELLS // 4)
-    def _(j):
-        r = pl.multiple_of(j * 512, 512)
-        even = dot_nt(qall[0], kp_ref[pl.ds(r, 256), :])
-        odd = dot_nt(qall[1], kp_ref[pl.ds(r + 256, 256), :])
-        for v in range(NQ // 8):
-            for h in range(2):
-                ev = even[v * 8 : v * 8 + 8, h * 128 : (h + 1) * 128]
-                od = odd[v * 8 : v * 8 + 8, h * 128 : (h + 1) * 128]
-                to = pl.multiple_of(v * 512 + j * 16 + h * 8, 8)
-                cost_ref[pl.ds(to, 8), :] = jnp.where(low, ev, od)
-                cost_ref[pl.ds(to + 256, 8), :] = jnp.where(low, od, ev)
+    @pl.loop(0, CELLS // 8)
+    def _(jj):
+        for u in range(2):
+            j = jj * 2 + u
+            r = pl.multiple_of(j * 512, 512)
+            even = dot_nt(qall[0], kp_ref[pl.ds(r, 256), :])
+            odd = dot_nt(qall[1], kp_ref[pl.ds(r + 256, 256), :])
+            for v in range(NQ // 8):
+                for h in range(2):
+                    ev = even[v * 8 : v * 8 + 8, h * 128 : (h + 1) * 128]
+                    od = odd[v * 8 : v * 8 + 8, h * 128 : (h + 1) * 128]
+                    to = pl.multiple_of(v * 512 + j * 16 + h * 8, 8)
+                    cost_ref[pl.ds(to, 8), :] = jnp.where(low, ev, od)
+                    cost_ref[pl.ds(to + 256, 8), :] = jnp.where(low, od, ev)
 
 
 def pipeline(mask_ref, wd_ref, bias_ref, gain_ref, smap_ref, w_ref, lse_ref, cost_ref, toks, nrms, ps, ms, after):
@@ -255,19 +259,28 @@
             )
             yield
 
-    @pl.loop(0, (NG + 3 + 2) // 3)
+    def block(g, u, order):
+        steps = {"w": sums(g, u), "s": scores(g, (u + 1) % 3), "n": norms((u + 2) % 3), "t": tokens(g, u)}
+        for step in order:
+            next(steps[step])
+
+    block(0, 0, "t" * 8)
+    block(1, 1, "tnnnn" * 8)
+    block(2, 2, "snn" * 4 + "tnnn" * 8)
+
+    @pl.loop(1, 7)
     def _(it):
         for u in range(3):
             g = it * 3 + u
 
-            @pl.when(g < NG + 3)
+            @pl.when(g < NG + 1)
             def _():
-                steps = {
-                    "w": sums(g, u), "s": scores(g, (u + 1) % 3), "n": norms((u + 2) % 3), "t": tokens(g, u),
-                }
-                for step in "w" + "n" * 16 + "snn" * 4 + "tn" * 8:
-                    next(steps[step])
+                block(g, u, "w" + "n" * 16 + "snn" * 4 + "tn" * 8)
                 after(g)
+
+    block(NG + 1, (NG + 1) % 3, "w" + "ssss")
+    block(NG + 2, (NG + 2) % 3, "w")
+    after(NG + 2)
 
 
 def split(a, n):
@@ -316,17 +329,17 @@
     y = lax.axis_index("ka")
     def prepare():
         parameters(weight_ref, pbias_ref, pgain_ref, latq_ref, key_ref, wd_ref, bias_ref, gain_ref, smap_ref)
-        for refs in (ps, ms, nrms, toks):
-            for ref in refs:
-                ref[...] = jnp.ones_like(ref)
 
     def queries():
         rows = jnp.concatenate([qbuf[i] for i in range(NY)], axis=0).astype(f32).T
         qall[0] = rows.astype(bf16)
         qall[1] = pltpu.roll(rows.reshape(NQ // 8, 8, CH), 4, 1).reshape(NQ, CH).astype(bf16)
 
-    gather(me, y, k_ref, q_ref, kbuf, qbuf, ssem, rsem, qssem, qrsem, prepare, queries)
-    order_keys(kbuf, kf_ref, kp_ref)
+    def landed(slot):
+        spread(slot, kbuf, kf_ref)
+
+    gather(me, y, k_ref, q_ref, kbuf, qbuf, ssem, rsem, qssem, qrsem, prepare, queries, landed)
+    order_keys(kf_ref, kp_ref)
     costs(qall, kp_ref, cost_ref)
     lane64 = lax.broadcasted_iota(jnp.int32, (64, 128), 1)
     lane8 = lax.broadcasted_iota(jnp.int32, (8, 128), 1)

time: 63.6 us -> 59.9 us (0.942)
  Pallas kernels: 61.7 us -> 58 us
    pallas_call x1, Pallas kernels: 61.7 us -> 58 us  [body(): pl.pallas_call(kernel, out_shape=jax.ShapeDtypeStruct((NQ, 2 * LD), bf16)...]
where the time goes in v3:
time: 59.9 us; the launch traced here: 59.8 us
  Pallas kernels  58 us (97%)
  local copies, waits for them, and re-layouts  1.78 us (3%)
    pallas_call x1, Pallas kernels, body(): pl.pallas_call(kernel, out_shape=jax.ShapeDtypeStruct((NQ, 2 * LD), bf16)...  58 us
    reshape x1, local copies, waits for them, and re-layouts, body(): return out.reshape(NQ, 2, LD)  1.78 us

profile of v3, /device:TPU:1, one launch (start us, length us, event | category | flops | bytes accessed | tf_op | source)
XLA Modules:
  0.0 59.8 jit_solution(1063030031145067070)
XLA Ops:
  0.0 58.0 %shard_map.91 = bf16[640,256]{1,0:T(8,128)(2,1)} custom-call(bf16[64,640]{1,0:T(8,128)(2,1)} %bitcast.3, bf16[128,256]{1,0:T(8,128)(2,1)} %k_ref.1, s32[640,128]{1,0:T(8,128)} %mask_ref.1, bf16[64,64]{1,0:T(8,128)(2,1)} %weight_ref.1, f32[1,64]{1,0:T(1,128)} %bitcast.4, f32[1,64]{1,0:T(1,128)} %bitcast.5, f32[8,128]{1,0:T(8,128)} %latq_ref.1, ...), custom_call_target="tpu_custom_call" | custom-call | tf_op jit(solution)/shard_map/pallas_call | solution.py:429
  58.0 1.8 %reshape.11 = bf16[640,2,128]{2,1,0:T(2,128)(2,1)} reshape(bf16[640,256]{1,0:T(8,128)(2,1)} %shard_map.91) | data formatting | bytes 655360 | tf_op jit(solution)/shard_map/reshape | solution.py:471

commit v4 on v3

--- a/solution.py
+++ b/solution.py
@@ -133,9 +133,12 @@
         copy(2 * i + 1 - core, sibling, 0).wait_recv()
         landed(2 * i + 1 - core)
 
-    @pl.loop(0, 63)
-    def _(i):
-        copy(me, sibling, i).wait_send()
+    def sent():
+        @pl.loop(0, 63)
+        def _(i):
+            copy(me, sibling, i).wait_send()
+
+    return sent
 
 
 def spread(slot, kbuf, kf_ref):
@@ -185,48 +188,47 @@
 
     def sums(g, slot):
         nrm_ref, p_ref, m_ref = nrms[slot], ps[slot], ms[slot]
-        b2 = lax.rem(g + 1, 2) * 2
-        zero = jnp.zeros((16, 128), bf16)
-        rows = []
-        for lp in range(LAT):
-            st = jnp.bitwise_xor(b2, lp)
-            pa = p_ref[pl.ds(st, 16, stride=8), :].astype(bf16)
-            pb = p_ref[pl.ds(st + 128, 16, stride=8), :].astype(bf16)
-            rows += [jnp.concatenate([pa, zero], axis=1), jnp.concatenate([zero, pb], axis=1)]
-        pst = jnp.concatenate(rows, axis=0)
-        o = dot_nt(jnp.concatenate([nrm_ref[...], jnp.ones((16, 256), bf16)], axis=0), pst)
-        acc = None
-        for p in range(NP):
-            ov = [o[p * 64 : (p + 1) * 64, v * 128 : (v + 1) * 128] for v in range(2)]
-            own = lax.bitwise_and(lane64, 15) == p
-            acc = ov if acc is None else [jnp.where(own, ov[v], acc[v]) for v in range(2)]
-        d = o[NP * 64 : NP * 64 + 1, :]
-        rd = 1.0 / d
-        for v in range(2):
-            vl = slice(v * 128, (v + 1) * 128)
-            w_ref[pl.ds(pl.multiple_of(g * 64, 64), 64), vl] = acc[v] * rd[:, vl]
-        lse_ref[pl.ds(pl.multiple_of(g * 8, 8), 8), :] = jnp.broadcast_to(m_ref[0:1, :] + jnp.log(d), (8, 256))
-        yield
+        b4 = lax.rem(g + 1, 2) * 4
+        zero = jnp.zeros((8, 128), f32)
+        for hh in range(2):
+            rows = []
+            for lp in range(LAT):
+                st = jnp.bitwise_xor(b4, lp ^ (2 * hh)) + hh * 128
+                pa = p_ref[pl.ds(st, 8, stride=8), :]
+                pb = p_ref[pl.ds(st + 64, 8, stride=8), :]
+                left, right = jnp.concatenate([pa, zero], axis=0), jnp.concatenate([zero, pb], axis=0)
+                rows.append(jnp.concatenate([left.astype(bf16), right.astype(bf16)], axis=1))
+            lhs = jnp.concatenate([nrm_ref[hh * 512 : hh * 512 + 512, :], jnp.ones((16, 256), bf16)], axis=0)
+            o = dot_nt(lhs, jnp.concatenate(rows, axis=0))
+            acc = o[0:64, :]
+            for p in range(1, 8):
+                acc = jnp.where(lax.bitwise_and(lane64, 7) == p, o[p * 64 : (p + 1) * 64, :], acc)
+            d = o[512:513, :]
+            vl = slice(hh * 128, (hh + 1) * 128)
+            w_ref[pl.ds(pl.multiple_of(g * 64, 64), 64), vl] = acc * (1.0 / d)
+            lse_ref[pl.ds(pl.multiple_of(g * 8, 8), 8), vl] = jnp.broadcast_to(m_ref[0:1, vl] + jnp.log(d), (8, 128))
+            yield
 
     def scores(g, slot):
         nrm_ref, p_ref, m_ref = nrms[slot], ps[slot], ms[slot]
-        b2 = lax.rem(g, 2) * 2
-        pos = lane - lax.bitwise_and(jnp.bitwise_xor(sub, b2), 3) * 32
-        accm = jnp.zeros((8, 128), f32)
+        b4 = lax.rem(g, 2) * 4
+        pos = [lane - jnp.bitwise_xor(sub, b4 + 2 * hh) * 16 for hh in range(2)]
+        accm = [jnp.zeros((8, 128), f32)] * 2
         for k in range(NP // 4):
             s3 = jnp.dot(smap_ref[...], nrm_ref[k * 256 : (k + 1) * 256, :], preferred_element_type=f32)
             for i in range(4):
                 s = s3[24 * i : 24 * i + 8] + (s3[24 * i + 8 : 24 * i + 16] + s3[24 * i + 16 : 24 * i + 24])
                 for h in range(2):
-                    q = h * 16 + k * 4 + i
+                    hh, p = divmod(k * 4 + i, 8)
+                    q = hh * 16 + h * 8 + p
                     sq = s[:, h * 128 : (h + 1) * 128]
                     m = jnp.broadcast_to(jnp.max(sq, axis=1, keepdims=True), (8, 128))
                     p_ref[q * 8 : q * 8 + 8, :] = jnp.exp(sq - m)
-                    accm = jnp.where(pos == q, m, accm)
+                    accm[hh] = jnp.where(pos[hh] == h * 8 + p, m, accm[hh])
             if k < NP // 4 - 1:
                 yield
-        m_ref[:, 0:128] = jnp.broadcast_to(jnp.sum(jnp.where(sub < 4, accm, 0.0), axis=0, keepdims=True), (8, 128))
-        m_ref[:, 128:256] = jnp.broadcast_to(jnp.sum(jnp.where(sub < 4, 0.0, accm), axis=0, keepdims=True), (8, 128))
+        for hh in range(2):
+            m_ref[:, hh * 128 : (hh + 1) * 128] = jnp.broadcast_to(jnp.sum(accm[hh], axis=0, keepdims=True), (8, 128))
         yield
 
     def norms(slot):
@@ -247,7 +249,7 @@
             for i in range(2):
                 xs = []
                 for h in range(2):
-                    q = h * 16 + k * 2 + i
+                    q = (k * 2 + i) // 8 * 16 + h * 8 + (k * 2 + i) % 8
                     base = pl.multiple_of((q0 + q // 4 * 4) * CELLS, 256) + q % 4
                     xq = cost_ref[pl.ds(base, CELLS, stride=4), :].astype(bf16)
                     mk = jnp.broadcast_to(mask_ref[pl.ds(q0 + q, 1), :].astype(f32), (CELLS, NT)).astype(bf16)
@@ -275,11 +277,11 @@
 
             @pl.when(g < NG + 1)
             def _():
-                block(g, u, "w" + "n" * 16 + "snn" * 4 + "tn" * 8)
+                block(g, u, "wnnnnnnnn" * 2 + "snn" * 4 + "tn" * 8)
                 after(g)
 
-    block(NG + 1, (NG + 1) % 3, "w" + "ssss")
-    block(NG + 2, (NG + 2) % 3, "w")
+    block(NG + 1, (NG + 1) % 3, "ww" + "ssss")
+    block(NG + 2, (NG + 2) % 3, "ww")
     after(NG + 2)
 
 
@@ -338,7 +340,7 @@
     def landed(slot):
         spread(slot, kbuf, kf_ref)
 
-    gather(me, y, k_ref, q_ref, kbuf, qbuf, ssem, rsem, qssem, qrsem, prepare, queries, landed)
+    sent = gather(me, y, k_ref, q_ref, kbuf, qbuf, ssem, rsem, qssem, qrsem, prepare, queries, landed)
     order_keys(kf_ref, kp_ref)
     costs(qall, kp_ref, cost_ref)
     lane64 = lax.broadcasted_iota(jnp.int32, (64, 128), 1)
@@ -359,21 +361,22 @@
             ),
         )
 
+    def quarters(lane, a):
+        return jnp.where(lane < 64, jnp.where(lane < 32, a[0], a[1]), jnp.where(lane < 96, a[2], a[3]))
+
     def send_chunk(k):
         for blk in range(2):
             ga = k * GPC + blk * 2 + 3
-            for v in range(2):
-                vl = slice(v * 128, (v + 1) * 128)
-                wa = w_ref[pl.ds(pl.multiple_of(ga * 64, 64), 64), vl]
-                wb = w_ref[pl.ds(pl.multiple_of(ga * 64 + 64, 64), 64), vl]
-                la = lse_ref[pl.ds(pl.multiple_of(ga * 8, 8), 8), vl]
-                lb = lse_ref[pl.ds(pl.multiple_of(ga * 8 + 8, 8), 8), vl]
-                rows = pl.ds(pl.multiple_of(k * 128 + blk * 64, 64), 64)
-                st = pl.ds(pl.multiple_of(k * 16 + blk * 8, 8), 8)
-                sbuf[2 * v, rows, :] = jnp.where(lane64 < 64, wa, wb).astype(bf16)
-                sbuf[2 * v + 1, rows, :] = jnp.where(lane64 < 64, wb, wa).astype(bf16)
-                sst[2 * v, st, :] = jnp.where(lane8 < 64, la, lb)
-                sst[2 * v + 1, st, :] = jnp.where(lane8 < 64, lb, la)
+            rows = pl.ds(pl.multiple_of(k * 128 + blk * 64, 64), 64)
+            st = pl.ds(pl.multiple_of(k * 16 + blk * 8, 8), 8)
+            wr = [pl.ds(pl.multiple_of((ga + i) * 64, 64), 64) for i in range(2)]
+            lr = [pl.ds(pl.multiple_of((ga + i) * 8, 8), 8) for i in range(2)]
+            vl = [slice(hh * 128, (hh + 1) * 128) for hh in range(2)]
+            ws = [w_ref[wr[hg // 2], vl[hg % 2]] for hg in range(4)]
+            ls = [lse_ref[lr[hg // 2], vl[hg % 2]] for hg in range(4)]
+            for j in range(NY):
+                sbuf[j, rows, :] = quarters(lane64, [ws[j ^ i] for i in range(4)]).astype(bf16)
+                sst[j, st, :] = quarters(lane8, [ls[j ^ i] for i in range(4)])
         for o in range(1, NY):
             for c in copies(k, o):
                 c.start()
@@ -382,7 +385,6 @@
         for o in range(1, NY):
             for c in copies(k, o):
                 c.wait_recv()
-        odd = lax.rem(y, 2)
         for blk in range(2):
             rows = pl.ds(pl.multiple_of(k * 128 + blk * 64, 64), 64)
             st = pl.ds(pl.multiple_of(k * 16 + blk * 8, 8), 8)
@@ -395,12 +397,12 @@
             res = lax.dot_general(
                 pooled.astype(bf16), value_ref[...], (((0,), (0,)), ((), ())), preferred_element_type=f32
             ).astype(bf16)
-            for half in range(2):
-                off = odd * 32 if half == 0 else (1 - odd) * 32
-                orow = pl.ds(pl.multiple_of(k * 128 + blk * 64 + off, 32), 32)
+            for i in range(4):
+                off = jnp.bitwise_xor(y, i) * 16
+                orow = pl.ds(pl.multiple_of(k * 128 + blk * 64 + off, 16), 16)
                 for l in range(2):
-                    r = (half * 2 + l) * 32
-                    out_ref[orow, l * 128 : (l + 1) * 128] = res[r : r + 32, :]
+                    r = i * 32 + l * 16
+                    out_ref[orow, l * 128 : (l + 1) * 128] = res[r : r + 16, :]
 
     def after(g):
         @pl.when(jnp.logical_and(lax.rem(g, GPC) == 2, g > 3))
@@ -410,15 +412,15 @@
 
     pipeline(mask_ref, wd_ref, bias_ref, gain_ref, smap_ref, w_ref, lse_ref, cost_ref, toks, nrms, ps, ms, after)
 
-    @pl.loop(0, NCH)
-    def _(k):
-        combine_chunk(k)
-
-    @pl.loop(0, NCH)
-    def _(k):
+    def chunk_sent(k):
         for o in range(1, NY):
             for c in copies(k, o):
                 c.wait_send()
+
+    sent()
+    pl.loop(0, NCH - 1)(chunk_sent)
+    pl.loop(0, NCH)(combine_chunk)
+    chunk_sent(NCH - 1)
 
 
 def body(

time: 59.9 us -> 58.1 us (0.970)
  Pallas kernels: 58 us -> 56.2 us
    pallas_call x1, Pallas kernels: 58 us -> 56.2 us  [body(): pl.pallas_call(kernel, out_shape=jax.ShapeDtypeStruct((NQ, 2 * LD), bf16)...]
where the time goes in v4:
time: 58.1 us; the launch traced here: 58 us
  Pallas kernels  56.2 us (97%)
  local copies, waits for them, and re-layouts  1.78 us (3%)
    pallas_call x1, Pallas kernels, body(): pl.pallas_call(kernel, out_shape=jax.ShapeDtypeStruct((NQ, 2 * LD), bf16)...  56.2 us
    reshape x1, local copies, waits for them, and re-layouts, body(): return out.reshape(NQ, 2, LD)  1.78 us

profile of v4, /device:TPU:1, one launch (start us, length us, event | category | flops | bytes accessed | tf_op | source)
XLA Modules:
  0.0 58.0 jit_solution(18260351784084884079)
XLA Ops:
  0.0 56.2 %shard_map.91 = bf16[640,256]{1,0:T(8,128)(2,1)} custom-call(bf16[64,640]{1,0:T(8,128)(2,1)} %bitcast.3, bf16[128,256]{1,0:T(8,128)(2,1)} %k_ref.1, s32[640,128]{1,0:T(8,128)} %mask_ref.1, bf16[64,64]{1,0:T(8,128)(2,1)} %weight_ref.1, f32[1,64]{1,0:T(1,128)} %bitcast.4, f32[1,64]{1,0:T(1,128)} %bitcast.5, f32[8,128]{1,0:T(8,128)} %latq_ref.1, ...), custom_call_target="tpu_custom_call" | custom-call | tf_op jit(solution)/shard_map/pallas_call | solution.py:431
  56.2 1.8 %reshape.11 = bf16[640,2,128]{2,1,0:T(2,128)(2,1)} reshape(bf16[640,256]{1,0:T(8,128)(2,1)} %shard_map.91) | data formatting | bytes 655360 | tf_op jit(solution)/shard_map/reshape | solution.py:473

commit v5 on v4

--- a/solution.py
+++ b/solution.py
@@ -165,10 +165,10 @@
 def costs(qall, kp_ref, cost_ref):
     low = lax.broadcasted_iota(jnp.int32, (8, 128), 0) < 4
 
-    @pl.loop(0, CELLS // 8)
+    @pl.loop(0, CELLS // 16)
     def _(jj):
-        for u in range(2):
-            j = jj * 2 + u
+        for u in range(4):
+            j = jj * 4 + u
             r = pl.multiple_of(j * 512, 512)
             even = dot_nt(qall[0], kp_ref[pl.ds(r, 256), :])
             odd = dot_nt(qall[1], kp_ref[pl.ds(r + 256, 256), :])

time: 58.1 us -> 57.3 us (0.986)
  Pallas kernels: 56.2 us -> 55.4 us
    pallas_call x1, Pallas kernels: 56.2 us -> 55.4 us  [body(): pl.pallas_call(kernel, out_shape=jax.ShapeDtypeStruct((NQ, 2 * LD), bf16)...]
where the time goes in v5:
time: 57.3 us; the launch traced here: 57.2 us
  Pallas kernels  55.4 us (97%)
  local copies, waits for them, and re-layouts  1.78 us (3%)
    pallas_call x1, Pallas kernels, body(): pl.pallas_call(kernel, out_shape=jax.ShapeDtypeStruct((NQ, 2 * LD), bf16)...  55.4 us
    reshape x1, local copies, waits for them, and re-layouts, body(): return out.reshape(NQ, 2, LD)  1.78 us

profile of v5, /device:TPU:1, one launch (start us, length us, event | category | flops | bytes accessed | tf_op | source)
XLA Modules:
  0.0 57.2 jit_solution(4392896100945943389)
XLA Ops:
  0.0 55.4 %shard_map.91 = bf16[640,256]{1,0:T(8,128)(2,1)} custom-call(bf16[64,640]{1,0:T(8,128)(2,1)} %bitcast.3, bf16[128,256]{1,0:T(8,128)(2,1)} %k_ref.1, s32[640,128]{1,0:T(8,128)} %mask_ref.1, bf16[64,64]{1,0:T(8,128)(2,1)} %weight_ref.1, f32[1,64]{1,0:T(1,128)} %bitcast.4, f32[1,64]{1,0:T(1,128)} %bitcast.5, f32[8,128]{1,0:T(8,128)} %latq_ref.1, ...), custom_call_target="tpu_custom_call" | custom-call | tf_op jit(solution)/shard_map/pallas_call | solution.py:431
  55.4 1.8 %reshape.11 = bf16[640,2,128]{2,1,0:T(2,128)(2,1)} reshape(bf16[640,256]{1,0:T(8,128)(2,1)} %shard_map.91) | data formatting | bytes 655360 | tf_op jit(solution)/shard_map/reshape | solution.py:473
